TPU v7x, 32 devices: a whole 2x2x4 slice. The times are simulated.
32 devices in a mesh: img: 8 (over y, x, core), row: 4 (over z).
Axes of the slice: x: 2, y: 2, z: 4, core: 2. Of those that a mesh axis runs over, the one named last changes fastest.
Arguments:
- latents: bfloat16 [64, 512, 1024], P('img', 'row'), may hold values from -6 to 6
- cotangent: bfloat16 [64, 512, 1024], P('img', 'row'), may hold values from -6 to 6
- slot_crops: int32 [64], P('img'), may hold values from 0 to 8, as said below
- ln1_scale: bfloat16 [1024], replicated, may hold values from 0.25 to 1.75
- ln1_offset: bfloat16 [1024], replicated, may hold values from -1.5 to 1.5
- qkv_weight: bfloat16 [1024, 3072], replicated, may hold values from -0.25 to 0.25
- out_weight: bfloat16 [1024, 1024], replicated, may hold values from -0.5 to 0.5
- out_bias: bfloat16 [1024], replicated, may hold values from -1.5 to 1.5
- ln2_scale: bfloat16 [1024], replicated, may hold values from 0.25 to 1.75
- ln2_offset: bfloat16 [1024], replicated, may hold values from -1.5 to 1.5
- up_weight: bfloat16 [1024, 1024], replicated, may hold values from -0.1875 to 0.1875
- up_bias: bfloat16 [1024], replicated, may hold values from -2.5 to 2.5
- down_weight: bfloat16 [1024, 1024], replicated, may hold values from -0.25 to 0.25
- down_bias: bfloat16 [1024], replicated, may hold values from -1.5 to 1.5
Outputs:
- block_out: bfloat16 [64, 512, 1024], P('img', 'row')
- latents_grad: bfloat16 [64, 512, 1024], P('img', 'row')
- ln1_scale_grad: float32 [1024], P(('img', 'row'))
- ln1_offset_grad: float32 [1024], P(('img', 'row'))
- qkv_weight_grad: float32 [1024, 3072], P(('img', 'row'))
- out_weight_grad: float32 [1024, 1024], P(('img', 'row'))
- out_bias_grad: float32 [1024], P(('img', 'row'))
- ln2_scale_grad: float32 [1024], P(('img', 'row'))
- ln2_offset_grad: float32 [1024], P(('img', 'row'))
- up_weight_grad: float32 [1024, 1024], P(('img', 'row'))
- up_bias_grad: float32 [1024], P(('img', 'row'))
- down_weight_grad: float32 [1024, 1024], P(('img', 'row'))
- down_bias_grad: float32 [1024], P(('img', 'row'))
Inputs may be any that keep to these rules, and one draw needn't show every extreme that they name: `slot_crops`: A slot holds the number of crops of its image, 1 to 8, or 0 if it is empty. The full slots, in slot order, hold the images one after another, each image's crops in consecutive full slots; the first image has 8 crops in every draw. Each index of img holds at least one full slot, its empty slots stand after its full ones, the first index of img has no empty slot and the last at least one.
All inputs are finite; a program needn't handle non-finite values.
Results may differ from a plain program's by a relative error of at most 0.015.
Values may be sent and summed in bfloat16 or wider, within the bound.
A program may use at most 256 MiB of HBM per device.

v0:
```python
import jax
import jax.numpy as jnp
from jax import lax
from jax.sharding import PartitionSpec as P

HEADS = 8


EPSILON = 1e-05


def norm_forward(values, scale, offset):
    row_mean = jnp.mean(values, -1, keepdims=True)
    centred = values - row_mean
    inverse = lax.rsqrt(jnp.mean(centred * centred, -1, keepdims=True) + EPSILON)
    normed = centred * inverse
    return (normed * scale + offset, normed, inverse)


def norm_backward(upstream, normed, inverse, scale):
    scaled = upstream * scale
    centre = (
        scaled
        - jnp.mean(scaled, -1, keepdims=True)
        - normed * jnp.mean(scaled * normed, -1, keepdims=True)
    )
    return (inverse * centre, jnp.sum(upstream * normed, 0), jnp.sum(upstream, 0))


def outer_total(left, right):
    return lax.dot_general(
        left, right, (((0,), (0,)), ((), ())), preferred_element_type=jnp.float32
    )


def back_product(upstream, weight):
    return lax.dot_general(
        upstream, weight, (((1,), (1,)), ((), ())), preferred_element_type=jnp.float32
    )


def soft_rows(scores):
    row_top = jnp.max(scores, -1, keepdims=True)
    expanded = jnp.exp(scores - row_top)
    return expanded / jnp.sum(expanded, -1, keepdims=True)


def local(
    latents,
    cotangent,
    slot_crops,
    ln1_scale,
    ln1_offset,
    qkv_weight,
    out_weight,
    out_bias,
    ln2_scale,
    ln2_offset,
    up_weight,
    up_bias,
    down_weight,
    down_bias,
):
    slot_count, row_count, feature_dim = latents.shape
    head_size = feature_dim // HEADS
    factor = head_size ** (-0.5)
    flat_rows = slot_count * row_count
    first_scale = ln1_scale.astype(jnp.float32)
    second_scale = ln2_scale.astype(jnp.float32)
    inputs_flat = latents.astype(jnp.float32).reshape(flat_rows, feature_dim)
    first_out, first_hat, first_inv = norm_forward(
        inputs_flat, first_scale, ln1_offset.astype(jnp.float32)
    )
    hidden_one = first_out.astype(jnp.bfloat16)
    qkv = jnp.dot(hidden_one, qkv_weight, preferred_element_type=jnp.float32).astype(jnp.bfloat16)
    query_flat = qkv[:, :feature_dim].reshape(slot_count, row_count, feature_dim)
    queries = query_flat.reshape(slot_count, row_count, HEADS, head_size)
    key_local = qkv[:, feature_dim : 2 * feature_dim].reshape(slot_count, row_count, feature_dim)
    value_local = qkv[:, 2 * feature_dim :].reshape(slot_count, row_count, feature_dim)
    key_whole, value_whole = (
        lax.all_gather(key_local, "row", axis=1, tiled=True),
        lax.all_gather(value_local, "row", axis=1, tiled=True),
    )
    crop_rows = key_whole.shape[1]
    key_whole = key_whole.reshape(slot_count, crop_rows, HEADS, head_size)
    value_whole = value_whole.reshape(slot_count, crop_rows, HEADS, head_size)
    scores = (
        jnp.einsum("srhd,skhd->shrk", queries, key_whole, preferred_element_type=jnp.float32)
        * factor
    )
    probs = soft_rows(scores)
    probs_low = probs.astype(jnp.bfloat16)
    mixed = jnp.einsum(
        "shrk,skhd->srhd", probs_low, value_whole, preferred_element_type=jnp.float32
    )
    mixed_low = mixed.reshape(flat_rows, feature_dim).astype(jnp.bfloat16)
    attended = jnp.dot(mixed_low, out_weight, preferred_element_type=jnp.float32) + out_bias.astype(
        jnp.float32
    )
    resid = inputs_flat + attended
    second_out, second_hat, second_inv = norm_forward(
        resid, second_scale, ln2_offset.astype(jnp.float32)
    )
    hidden_two = second_out.astype(jnp.bfloat16)
    before = jnp.dot(hidden_two, up_weight, preferred_element_type=jnp.float32) + up_bias.astype(
        jnp.float32
    )
    activated, gelu_pull = jax.vjp(jax.nn.gelu, before)
    act_low = activated.astype(jnp.bfloat16)
    branch = jnp.dot(act_low, down_weight, preferred_element_type=jnp.float32) + down_bias.astype(
        jnp.float32
    )
    valid = slot_crops > 0
    result = (resid + branch).reshape(slot_count, row_count, feature_dim)
    block_out = jnp.where(valid[:, None, None], result, 0.0).astype(jnp.bfloat16)
    share = jnp.where(valid, 1.0 / jnp.maximum(slot_crops, 1).astype(jnp.float32), 0.0)
    grad_out = (cotangent.astype(jnp.float32) * share[:, None, None]).reshape(
        flat_rows, feature_dim
    )
    grad_low = grad_out.astype(jnp.bfloat16)
    down_grad = outer_total(act_low, grad_low)
    down_bias_grad = jnp.sum(grad_low.astype(jnp.float32), 0)
    grad_act = back_product(grad_low, down_weight)
    grad_before = gelu_pull(grad_act)[0].astype(jnp.bfloat16)
    up_grad = outer_total(hidden_two, grad_before)
    up_bias_grad = jnp.sum(grad_before.astype(jnp.float32), 0)
    grad_hidden_two = back_product(grad_before, up_weight)
    resid_part, second_scale_grad, second_offset_grad = norm_backward(
        grad_hidden_two, second_hat, second_inv, second_scale
    )
    grad_resid = grad_out + resid_part
    grad_attn = grad_resid.astype(jnp.bfloat16)
    out_grad = outer_total(mixed_low, grad_attn)
    out_bias_grad = jnp.sum(grad_attn.astype(jnp.float32), 0)
    grad_mixed_flat = (
        back_product(grad_attn, out_weight)
        .astype(jnp.bfloat16)
        .reshape(slot_count, row_count, feature_dim)
    )
    grad_mixed = grad_mixed_flat.reshape(slot_count, row_count, HEADS, head_size)
    grad_probs = jnp.einsum(
        "srhd,skhd->shrk", grad_mixed, value_whole, preferred_element_type=jnp.float32
    )
    row_inner = jnp.sum(probs * grad_probs, -1, keepdims=True)
    grad_scores = (probs * (grad_probs - row_inner)).astype(jnp.bfloat16)
    query_grad = (
        jnp.einsum("shrk,skhd->srhd", grad_scores, key_whole, preferred_element_type=jnp.float32)
        * factor
    )
    count = lax.axis_size("row") * row_count
    key_part = (
        jnp.einsum("shrk,srhd->kshd", grad_scores, queries, preferred_element_type=jnp.float32)
        * factor
    )
    value_part = jnp.einsum(
        "shrk,srhd->kshd", probs_low, grad_mixed, preferred_element_type=jnp.float32
    )
    summed = lax.psum_scatter(
        jnp.concatenate(
            [
                key_part.reshape(count, slot_count * feature_dim),
                value_part.reshape(count, slot_count * feature_dim),
            ],
            1,
        ).astype(jnp.bfloat16),
        "row",
        scatter_dimension=0,
        tiled=True,
    ).astype(jnp.float32)
    key_grad = jnp.swapaxes(
        summed[:, : slot_count * feature_dim].reshape(row_count, slot_count, feature_dim), 0, 1
    )
    value_grad = jnp.swapaxes(
        summed[:, slot_count * feature_dim :].reshape(row_count, slot_count, feature_dim), 0, 1
    )
    grad_qkv = jnp.concatenate(
        [
            query_grad.reshape(flat_rows, feature_dim),
            key_grad.reshape(flat_rows, feature_dim),
            value_grad.reshape(flat_rows, feature_dim),
        ],
        1,
    ).astype(jnp.bfloat16)
    qkv_grad = outer_total(hidden_one, grad_qkv)
    grad_hidden_one = back_product(grad_qkv, qkv_weight)
    input_part, first_scale_grad, first_offset_grad = norm_backward(
        grad_hidden_one, first_hat, first_inv, first_scale
    )
    latents_grad = (
        (grad_resid + input_part).reshape(slot_count, row_count, feature_dim).astype(jnp.bfloat16)
    )
    totals = (
        lax.psum_scatter(first_scale_grad, ("img", "row"), scatter_dimension=0, tiled=True),
        lax.psum_scatter(first_offset_grad, ("img", "row"), scatter_dimension=0, tiled=True),
        lax.psum_scatter(qkv_grad, ("img", "row"), scatter_dimension=0, tiled=True),
        lax.psum_scatter(out_grad, ("img", "row"), scatter_dimension=0, tiled=True),
        lax.psum_scatter(out_bias_grad, ("img", "row"), scatter_dimension=0, tiled=True),
        lax.psum_scatter(second_scale_grad, ("img", "row"), scatter_dimension=0, tiled=True),
        lax.psum_scatter(second_offset_grad, ("img", "row"), scatter_dimension=0, tiled=True),
        lax.psum_scatter(up_grad, ("img", "row"), scatter_dimension=0, tiled=True),
        lax.psum_scatter(up_bias_grad, ("img", "row"), scatter_dimension=0, tiled=True),
        lax.psum_scatter(down_grad, ("img", "row"), scatter_dimension=0, tiled=True),
        lax.psum_scatter(down_bias_grad, ("img", "row"), scatter_dimension=0, tiled=True),
    )
    return (block_out, latents_grad) + tuple(totals)


def solution(mesh):
    in_specs = (
        P("img", "row", None),
        P("img", "row", None),
        P("img"),
        P(),
        P(),
        P(),
        P(),
        P(),
        P(),
        P(),
        P(),
        P(),
        P(),
        P(),
    )
    out_specs = (
        P("img", "row", None),
        P("img", "row", None),
        P(("img", "row")),
        P(("img", "row")),
        P(("img", "row"), None),
        P(("img", "row"), None),
        P(("img", "row")),
        P(("img", "row")),
        P(("img", "row")),
        P(("img", "row"), None),
        P(("img", "row")),
        P(("img", "row"), None),
        P(("img", "row")),
    )
    return jax.shard_map(local, mesh=mesh, in_specs=in_specs, out_specs=out_specs, check_vma=False)
```

profile of v0, /device:TPU:0, one launch (start us, length us, event | category | flops | bytes accessed | tf_op | source)
XLA Modules:
  0.0 1366.0 jit_solution(3689320609210338248)
XLA Ops:
  16.4 7.0 convolution_convert_fusion.1
  26.3 4.0 copy.57
  34.9 4.1 copy.64
  45.9 136.3 %all-gather.5.cloned.1.call-done = bf16[8,512,1024]{1,2,0:T(8,128)(2,1)} async-done(((bf16[8,128,1024]{1,2,0:T(8,128)(2,1)}), bf16[8,512,1024]{1,2,0:T(8,128)(2,1)}) %all-gather.5.cloned.1.call-update) | async-done | bytes 8388624 | tf_op jit(solution)/shard_map/all_gather | solution.py:81
  182.3 12.5 fusion.57
  194.8 136.9 %all-gather.3.cloned.1.call-done = bf16[8,512,1024]{2,1,0:T(8,128)(2,1)} async-done(((bf16[8,128,1024]{2,1,0:T(8,128)(2,1)}), bf16[8,512,1024]{2,1,0:T(8,128)(2,1)}) %all-gather.3.cloned.1.call-update) | async-done | bytes 8388624 | tf_op jit(solution)/shard_map/all_gather | solution.py:82
  331.7 11.4 copy.56
  343.1 11.0 convert_bitcast_fusion.1
  354.0 4.1 copy.60
  358.1 5.3 fusion.58
  367.2 6.1 convert_reduce_fusion.2
  385.2 10.7 convolution_convert_fusion
  395.9 15.1 %multiply_reduce_fusion = (f32[8,8,128]{2,1,0:T(8,128)S(1)}, f32[8,8,128,512]{3,2,1,0:T(8,128)}) fusion(f32[8,8,128,512]{3,2,1,0:T(8,128)} %get-tuple-element.42, f32[8,8,128]{2,1,0:T(8,128)S(1)} %get-tuple-element.41, bf16[8,128,8,128]{1,3,2,0:T(8,128)(2,1)S(1)} %copy-done.17, bf16[8,512,8,128]{1,3,2,0:T(8,128)(2,1)} %bitcast.116), kind=kOutput, calls=%fused_computation.4 | convolution fusion | flops 1086316544 | bytes 44105728 | tf_op jit(solution)/shard_map/srhd,skhd->shrk/dot_general | solution.py:141
  411.1 11.7 multiply_convert_fusion.1
  422.8 5.7 multiply_convert_fusion
  428.6 18.5 %pad_maximum_fusion = bf16[512,16384]{0,1:T(8,128)(2,1)} fusion(bf16[512,8192]{0,1:T(8,128)(2,1)} %bitcast.124, bf16[512,8192]{0,1:T(8,128)(2,1)} %bitcast.114), kind=kLoop, calls=%fused_computation.1 | loop fusion | flops 33554432 | bytes 33554432 | tf_op jit(solution)/shard_map/concatenate | solution.py:159
  447.0 21.2 %copy.70 = bf16[512,16384]{1,0:T(8,128)(2,1)} copy(bf16[512,16384]{0,1:T(8,128)(2,1)} %pad_maximum_fusion) | data formatting | bytes 33554432
  469.8 7.2 fusion.51
  478.7 6.7 fusion.52
  487.0 6.6 fusion.34
  493.6 8.1 fusion.44
  508.1 238.8 %reduce-scatter.16.cloned.1.call-done = bf16[128,16384]{1,0:T(8,128)(2,1)} async-done(((bf16[512,16384]{1,0:T(8,128)(2,1)}), bf16[128,16384]{1,0:T(8,128)(2,1)}) %reduce-scatter.16.cloned.1.call-update) | async-done | bytes 4194320
  746.9 4.7 fusion.56
  763.3 13.1 fusion.32
  778.0 6.5 add_add_fusion
  787.6 11.8 fusion.26
  799.4 42.2 %all-reduce.7 = (f32[1024]{0:T(1024)S(1)}, f32[1024]{0:T(1024)S(1)}, f32[1024]{0:T(1024)S(1)}, f32[1024]{0:T(1024)S(1)}, f32[1024]{0:T(1024)S(1)}, /*index=5*/f32[1024]{0:T(1024)S(1)}, f32[1024]{0:T(1024)S(1)}) all-reduce(f32[1024]{0:T(1024)S(1)} %get-tuple-element.15, ...), channel_id=3, replica_groups=mesh['img'=8,'row'=4] {'img','row'}, use_global_device_ids=true, to_apply=%region_13.14.clone | all-reduce | flops 7168 | bytes 57344
  845.7 6.0 fusion.25
  851.7 46.6 %reduce-scatter.14.cloned.1.call-done = f32[32,1024]{1,0:T(8,128)} async-done(((f32[1024,1024]{1,0:T(8,128)}), f32[32,1024]{1,0:T(8,128)}) %reduce-scatter.14.cloned.1.call-update) | async-done | bytes 131088 | tf_op jit(solution)/shard_map/reduce_scatter | solution.py:202
  898.3 148.7 %reduce-scatter.12.cloned.1.call-done = f32[32,1024]{1,0:T(8,128)} async-done(((f32[1024,1024]{1,0:T(8,128)}), f32[32,1024]{1,0:T(8,128)}) %reduce-scatter.12.cloned.1.call-update) | async-done | bytes 131088 | tf_op jit(solution)/shard_map/reduce_scatter | solution.py:200
  1046.9 150.0 %reduce-scatter.10.cloned.1.call-done = f32[32,1024]{1,0:T(8,128)} async-done(((f32[1024,1024]{1,0:T(8,128)}), f32[32,1024]{1,0:T(8,128)}) %reduce-scatter.10.cloned.1.call-update) | async-done | bytes 131088 | tf_op jit(solution)/shard_map/reduce_scatter | solution.py:196
  1196.9 161.7 %reduce-scatter.8.cloned.1.call-done = f32[32,3072]{1,0:T(8,128)} async-done(((f32[1024,3072]{1,0:T(8,128)}), f32[32,3072]{1,0:T(8,128)}) %reduce-scatter.8.cloned.1.call-update) | async-done | bytes 393232 | tf_op jit(solution)/shard_map/reduce_scatter | solution.py:195
  (144 shorter events, 70.5 us)
Async XLA Ops:
  7.2 356.9 %copy-start = (bf16[1024,1024]{1,0:T(8,128)(2,1)S(1)}, bf16[1024,1024]{1,0:T(8,128)(2,1)}, u32[]{:S(2)}) copy-start(bf16[1024,1024]{1,0:T(8,128)(2,1)} %param.24) | copy-start | bytes 6291460
  7.2 175.1 %all-gather.5.cloned.1.call-start = ((), (), s32[]{:S(2)}) async-start(), calls=%async_computation.6 | async-start | bytes 10485760 | tf_op jit(solution)/shard_map/all_gather | solution.py:81
  7.2 7.0 copy-start.5
  8.1 5.5 copy-start.20
  8.9 7.5 copy-start.34
  26.3 5.0 copy-start.29
  26.3 5.0 copy-start.30
  26.3 5.0 copy-start.31
  26.3 5.1 copy-start.32
  30.3 301.4 %all-gather.3.cloned.1.call-start = ((), (), s32[]{:S(2)}) async-start(), calls=%async_computation.5 | async-start | bytes 10485760 | tf_op jit(solution)/shard_map/all_gather | solution.py:82
  31.0 715.9 %reduce-scatter.16.cloned.1.call-start = ((), (), s32[]{:S(2)}) async-start(), calls=%async_computation.11 | async-start | bytes 20971520
  31.4 7.7 copy-start.38
  363.4 13.4 copy-start.9
  367.2 6.1 copy-start.40
  385.2 10.7 copy-start.17
  411.1 11.7 copy-start.7
  422.8 5.7 copy-start.2
  468.3 430.0 %reduce-scatter.14.cloned.1.call-start = ((), (), s32[]{:S(2)}) async-start(), calls=%async_computation.10 | async-start | bytes 4325376 | tf_op jit(solution)/shard_map/reduce_scatter | solution.py:202
  477.1 569.8 %reduce-scatter.12.cloned.1.call-start = ((), (), s32[]{:S(2)}) async-start(), calls=%async_computation.9 | async-start | bytes 4325376 | tf_op jit(solution)/shard_map/reduce_scatter | solution.py:200
  485.4 711.5 %reduce-scatter.10.cloned.1.call-start = ((), (), s32[]{:S(2)}) async-start(), calls=%async_computation.8 | async-start | bytes 4325376 | tf_op jit(solution)/shard_map/reduce_scatter | solution.py:196
  493.6 865.1 %reduce-scatter.8.cloned.1.call-start = ((), (), s32[]{:S(2)}) async-start(), calls=%async_computation.7 | async-start | bytes 12976128 | tf_op jit(solution)/shard_map/reduce_scatter | solution.py:195
  778.0 8.6 copy-start.15
  778.0 8.6 copy-start.16
  778.0 8.6 copy-start.19
  778.0 8.6 copy-start.21
  778.0 8.6 copy-start.23
  787.6 11.8 copy-start.24
  787.6 11.8 copy-start.25
  787.6 11.8 copy-start.26
  787.6 11.8 copy-start.27
  787.6 11.8 copy-start.28
  845.7 513.0 %copy-start.1 = (bf16[1024,1024]{1,0:T(8,128)(2,1)S(1)}, bf16[1024,1024]{1,0:T(8,128)(2,1)}, u32[]{:S(2)}) copy-start(bf16[1024,1024]{1,0:T(8,128)(2,1)} %param.24) | copy-start | bytes 6291460
  (18 other events, 37.0 us)
Sparse Core Ops, SparseCore 0:
  30.4 151.8 all-gather.4
  183.8 147.8 all-gather.2
  468.4 278.4 reduce-scatter.15
  749.7 148.4 reduce-scatter.13
  901.1 145.8 reduce-scatter.11
  1049.7 147.1 reduce-scatter.9
  1204.6 154.0 reduce-scatter.7
where the time goes:
time: 1370 us
  waiting for transfers between devices  1020 us (74%)
  matrix products  142 us (10%)
  local copies, waits for them, and re-layouts  92.9 us (7%)
  other arithmetic  53.4 us (4%)
  blocking collectives  42.2 us (3%)
  between operations  15.1 us (1%)
    unnamed x8, waiting for transfers between devices  240 us
    reduce_scatter x1, waiting for transfers between devices, local(): lax.psum_scatter(qkv_grad, ('img', 'row'), scatter_dimension=0, tiled=True)  162 us
    reduce_scatter x1, waiting for transfers between devices, local(): lax.psum_scatter(out_grad, ('img', 'row'), scatter_dimension=0, tiled=True)  150 us
    reduce_scatter x1, waiting for transfers between devices, local(): lax.psum_scatter(up_grad, ('img', 'row'), scatter_dimension=0, tiled=True)  149 us
    all_gather x1, waiting for transfers between devices, local(): lax.all_gather(value_local, 'row', axis=1, tiled=True)  137 us
    all_gather x1, waiting for transfers between devices, local(): lax.all_gather(key_local, 'row', axis=1, tiled=True)  136 us
    unnamed x99, local copies, waits for them, and re-layouts  50.9 us
    reduce_scatter x1, waiting for transfers between devices, local(): lax.psum_scatter(down_grad, ('img', 'row'), scatter_dimension=0, tiled=True)  46.6 us
  transfers between devices with their start and end apart: 7, of which 7 were waited for; matrix products, arithmetic and copies ran while one was open for 9% of the time, Pallas kernels for 0%

commit v1 on v0

v1 whole, which is shorter than its diff:
```python
import functools
import jax
import jax.numpy as jnp
from jax import lax
from jax.experimental import pallas as pl
from jax.experimental.pallas import tpu as pltpu
from jax.sharding import PartitionSpec as P

HEADS = 8
EPSILON = 1e-05
F32 = jnp.float32
BF16 = jnp.bfloat16
ANY = pl.BlockSpec(memory_space=pl.ANY)
VM = pl.BlockSpec(memory_space=pltpu.VMEM)
SM = pl.BlockSpec(memory_space=pltpu.SMEM)
VMEM_LIMIT = 60 * 1024 * 1024


def dot(a, b):
    return jnp.dot(a, b, preferred_element_type=F32)


def dot_t(a, b):
    return lax.dot_general(a, b, (((1,), (1,)), ((), ())), preferred_element_type=F32)


def dot_tt(a, b):
    return lax.dot_general(a, b, (((0,), (0,)), ((), ())), preferred_element_type=F32)


def norm_parts(values):
    mean = jnp.mean(values, -1, keepdims=True)
    centred = values - mean
    inverse = lax.rsqrt(jnp.mean(centred * centred, -1, keepdims=True) + EPSILON)
    return centred * inverse, inverse


GELU_A = 0.7978845608028654
GELU_B = 0.044715


def forward_kernel(
    pieces, rows, width,
    *refs,
):
    (full,), refs = refs[:1], refs[1:]
    xs, refs = refs[:pieces], refs[pieces:]
    (scale1, offset1, scale2, offset2, bias_o, bias_u, bias_d, w_qkv, w_o, w_u, w_d), refs = refs[:11], refs[11:]
    outs, refs = refs[:pieces], refs[pieces:]
    (h1_o, qkv_o, probs_o, mixed_o, resid_o, h2_o, pre_o, act_o), refs = refs[:8], refs[8:]
    (vq, vo, vu, vd, h1, qkv, probs, mixed, resid, h2, pre, act, in_sem, out_sem) = refs
    heads = HEADS
    size = width // heads
    chunk = rows // pieces
    loads = [
        pltpu.make_async_copy(a, b, in_sem.at[i])
        for i, (a, b) in enumerate(((w_qkv, vq), (w_o, vo), (w_u, vu), (w_d, vd)))
    ]
    for load in loads:
        load.start()
    saves = [
        pltpu.make_async_copy(a, b, out_sem.at[i])
        for i, (a, b) in enumerate(
            ((h1, h1_o), (qkv, qkv_o), (probs, probs_o), (mixed, mixed_o), (resid, resid_o), (h2, h2_o), (pre, pre_o), (act, act_o))
        )
    ]
    s1, o1 = scale1[...].astype(F32), offset1[...].astype(F32)
    for i, x in enumerate(xs):
        hat, _ = norm_parts(x[...].astype(F32))
        h1[pl.ds(i * chunk, chunk), :] = (hat * s1 + o1).astype(BF16)
    saves[0].start()
    loads[0].wait()

    @pl.loop(0, 3 * width // 256)
    def _(n):
        cols = pl.ds(pl.multiple_of(n * 256, 256), 256)
        qkv[:, cols] = dot(h1[...], vq[:, cols]).astype(BF16)

    saves[1].start()
    factor = size ** -0.5 * 1.4426950408889634

    for h in range(heads):
        q = qkv[:, h * size:(h + 1) * size]
        k = qkv[:, width + h * size:width + (h + 1) * size]
        v = qkv[:, 2 * width + h * size:2 * width + (h + 1) * size]
        s = dot_t(k, q)
        top = jnp.max(s, 0, keepdims=True)
        e = jnp.exp2((s - top) * factor)
        p = (e * (1.0 / jnp.sum(e, 0, keepdims=True))).astype(BF16)
        probs[h] = p
        o = dot(v.T, p)
        mixed[:, h * size:(h + 1) * size] = o.T.astype(BF16)
    saves[2].start()
    saves[3].start()
    loads[1].wait()
    bo = bias_o[...].astype(F32)
    s2, o2 = scale2[...].astype(F32), offset2[...].astype(F32)
    for i, x in enumerate(xs):
        part = pl.ds(i * chunk, chunk)
        r = x[...].astype(F32) + dot(mixed[part, :], vo[...]) + bo
        resid[part, :] = r
        hat, _ = norm_parts(r)
        h2[part, :] = (hat * s2 + o2).astype(BF16)
    saves[4].start()
    saves[5].start()
    loads[2].wait()
    bu = bias_u[...].astype(F32)
    for i in range(pieces):
        part = pl.ds(i * chunk, chunk)
        u = dot(h2[part, :], vu[...]) + bu
        pre[part, :] = u
        act[part, :] = (0.5 * u * (1.0 + jnp.tanh(GELU_A * (u + GELU_B * u * u * u)))).astype(BF16)
    saves[6].start()
    saves[7].start()
    loads[3].wait()
    bd = bias_d[...].astype(F32)
    keep = full[0] > 0
    for i in range(pieces):
        part = pl.ds(i * chunk, chunk)
        out = resid[part, :] + dot(act[part, :], vd[...]) + bd
        outs[i][...] = jnp.where(keep, out, 0.0).astype(BF16)
    for save in saves:
        save.wait()


def forward(full, xs, vecs, mats):
    pieces = len(xs)
    chunk, width = xs[0].shape
    rows = chunk * pieces
    sds = jax.ShapeDtypeStruct
    saved = [
        sds((rows, width), BF16), sds((rows, 3 * width), BF16), sds((HEADS, rows, rows), BF16), sds((rows, width), BF16),
        sds((rows, width), F32), sds((rows, width), BF16), sds((rows, width), F32), sds((rows, width), BF16),
    ]
    out_shape = [sds((chunk, width), BF16)] * pieces + saved
    macs = rows * width * width * 6 + 2 * rows * rows * width
    res = pl.pallas_call(
        functools.partial(forward_kernel, pieces, rows, width),
        out_shape=out_shape,
        in_specs=[SM] + [VM] * pieces + [VM] * 7 + [ANY] * 4,
        out_specs=[VM] * pieces + [ANY] * 8,
        scratch_shapes=[
            pltpu.VMEM((width, 3 * width), BF16), pltpu.VMEM((width, width), BF16), pltpu.VMEM((width, width), BF16), pltpu.VMEM((width, width), BF16),
        ] + [pltpu.VMEM(s.shape, s.dtype) for s in saved] + [pltpu.SemaphoreType.DMA((4,)), pltpu.SemaphoreType.DMA((8,))],
        compiler_params=pltpu.CompilerParams(vmem_limit_bytes=VMEM_LIMIT),
        cost_estimate=pl.CostEstimate(flops=2 * macs, bytes_accessed=32 << 20, transcendentals=0),
        name="slot_forward",
    )(full, *xs, *vecs, *mats)
    return res[:pieces], res[pieces:]


def backward_kernel(pieces, rows, width, *refs):
    (share,), refs = refs[:1], refs[1:]
    cots, refs = refs[:pieces], refs[pieces:]
    xs, refs = refs[:pieces], refs[pieces:]
    (scale1, scale2), refs = refs[:2], refs[2:]
    hbm_in, refs = refs[:9], refs[9:]
    outs, refs = refs[:pieces], refs[pieces:]
    (sums_o,), refs = refs[:1], refs[1:]
    (gl_o, gp_o, ga_o, gqkv_o), refs = refs[:4], refs[4:]
    (vd, pre, vu, resid, vo, qkv, probs, vq, _unused), refs = refs[:9], refs[9:]
    (gl, gp, ga, gqkv, gm, gres, sums, in_sem, out_sem) = refs
    size = width // HEADS
    chunk = rows // pieces
    vm_in = (vd, pre, vu, resid, vo, qkv, probs, vq)
    loads = [pltpu.make_async_copy(a, b, in_sem.at[i]) for i, (a, b) in enumerate(zip(hbm_in[:8], vm_in))]
    for load in loads:
        load.start()
    saves = [
        pltpu.make_async_copy(a, b, out_sem.at[i])
        for i, (a, b) in enumerate(((gl, gl_o), (gp, gp_o), (ga, ga_o), (gqkv, gqkv_o)))
    ]
    part_share = share[0]
    bias_d = jnp.zeros((1, width), F32)
    for i in range(pieces):
        part = pl.ds(i * chunk, chunk)
        g = (cots[i][...].astype(F32) * part_share).astype(BF16)
        gl[part, :] = g
        bias_d = bias_d + jnp.sum(g.astype(F32), 0, keepdims=True)
    sums[0:1, :] = bias_d
    saves[0].start()
    loads[0].wait()
    loads[1].wait()
    bias_u = jnp.zeros((1, width), F32)
    for i in range(pieces):
        part = pl.ds(i * chunk, chunk)
        ga_ = dot_t(gl[part, :], vd[...])
        u = pre[part, :]
        t = jnp.tanh(GELU_A * (u + GELU_B * u * u * u))
        slope = 0.5 * (1.0 + t) + 0.5 * u * (1.0 - t * t) * (GELU_A * (1.0 + 3.0 * GELU_B * u * u))
        g = (ga_ * slope).astype(BF16)
        gp[part, :] = g
        bias_u = bias_u + jnp.sum(g.astype(F32), 0, keepdims=True)
    sums[1:2, :] = bias_u
    saves[1].start()
    loads[2].wait()
    loads[3].wait()
    s2 = scale2[...].astype(F32)
    scale_g = jnp.zeros((1, width), F32)
    offset_g = jnp.zeros((1, width), F32)
    bias_o = jnp.zeros((1, width), F32)
    for i in range(pieces):
        part = pl.ds(i * chunk, chunk)
        gh = dot_t(gp[part, :], vu[...])
        hat, inverse = norm_parts(resid[part, :])
        scale_g = scale_g + jnp.sum(gh * hat, 0, keepdims=True)
        offset_g = offset_g + jnp.sum(gh, 0, keepdims=True)
        e = gh * s2
        gr = cots[i][...].astype(F32) * part_share + inverse * (
            e - jnp.mean(e, -1, keepdims=True) - hat * jnp.mean(e * hat, -1, keepdims=True)
        )
        gres[part, :] = gr
        g = gr.astype(BF16)
        ga[part, :] = g
        bias_o = bias_o + jnp.sum(g.astype(F32), 0, keepdims=True)
    sums[2:3, :] = scale_g
    sums[3:4, :] = offset_g
    sums[4:5, :] = bias_o
    saves[2].start()
    loads[4].wait()
    for i in range(pieces):
        part = pl.ds(i * chunk, chunk)
        gm[part, :] = dot_t(ga[part, :], vo[...]).astype(BF16)
    loads[5].wait()
    loads[6].wait()
    factor = size ** -0.5
    for h in range(HEADS):
        qc = slice(h * size, (h + 1) * size)
        kc = slice(width + h * size, width + (h + 1) * size)
        vc = slice(2 * width + h * size, 2 * width + (h + 1) * size)
        q, k, v, m = qkv[:, qc], qkv[:, kc], qkv[:, vc], gm[:, qc]
        p = probs[h]
        dp = dot_t(v, m)
        pf = p.astype(F32)
        w = pf * dp
        ds = (w - pf * jnp.sum(w, 0, keepdims=True)).astype(BF16)
        gqkv[:, vc] = dot(p, m).astype(BF16)
        gqkv[:, kc] = (dot(ds, q) * factor).astype(BF16)
        gqkv[:, qc] = (dot(k.T, ds) * factor).T.astype(BF16)
    saves[3].start()
    loads[7].wait()
    s1 = scale1[...].astype(F32)
    scale_g = jnp.zeros((1, width), F32)
    offset_g = jnp.zeros((1, width), F32)
    for i in range(pieces):
        part = pl.ds(i * chunk, chunk)
        gh = dot_t(gqkv[part, :], vq[...])
        hat, inverse = norm_parts(xs[i][...].astype(F32))
        scale_g = scale_g + jnp.sum(gh * hat, 0, keepdims=True)
        offset_g = offset_g + jnp.sum(gh, 0, keepdims=True)
        e = gh * s1
        outs[i][...] = (
            gres[part, :] + inverse * (e - jnp.mean(e, -1, keepdims=True) - hat * jnp.mean(e * hat, -1, keepdims=True))
        ).astype(BF16)
    sums[5:6, :] = scale_g
    sums[6:7, :] = offset_g
    sums[7:8, :] = jnp.zeros((1, width), F32)
    sums_o[...] = sums[...]
    for save in saves:
        save.wait()


def backward(share, cots, xs, vecs, hbm_in):
    pieces = len(xs)
    chunk, width = xs[0].shape
    rows = chunk * pieces
    sds = jax.ShapeDtypeStruct
    saved = [sds((rows, width), BF16), sds((rows, width), BF16), sds((rows, width), BF16), sds((rows, 3 * width), BF16)]
    macs = rows * width * width * 6 + 4 * rows * rows * width
    res = pl.pallas_call(
        functools.partial(backward_kernel, pieces, rows, width),
        out_shape=[sds((chunk, width), BF16)] * pieces + [sds((8, width), F32)] + saved,
        in_specs=[SM] + [VM] * (2 * pieces) + [VM] * 2 + [ANY] * 9,
        out_specs=[VM] * (pieces + 1) + [ANY] * 4,
        scratch_shapes=[pltpu.VMEM(a.shape, a.dtype) for a in hbm_in[:8]] + [pltpu.VMEM((8, 128), F32)]
        + [pltpu.VMEM(s.shape, s.dtype) for s in saved]
        + [pltpu.VMEM((rows, width), BF16), pltpu.VMEM((rows, width), F32), pltpu.VMEM((8, width), F32)]
        + [pltpu.SemaphoreType.DMA((8,)), pltpu.SemaphoreType.DMA((4,))],
        compiler_params=pltpu.CompilerParams(vmem_limit_bytes=VMEM_LIMIT),
        cost_estimate=pl.CostEstimate(flops=2 * macs, bytes_accessed=32 << 20, transcendentals=0),
        name="slot_backward",
    )(share, *cots, *xs, *vecs, *hbm_in)
    return res[:pieces], res[pieces], res[pieces + 1:]


def weight_kernel(count, half, quarters, *refs):
    (spots,), refs = refs[:1], refs[1:]
    lefts, refs = refs[: 2 * count], refs[2 * count:]
    rights, refs = refs[: 2 * count], refs[2 * count:]
    (left_kept, left_sent, right_kept, right_sent, turned) = refs
    step = pl.program_id(0)
    per = pl.num_programs(0) // count
    rows, width = lefts[0].shape
    blocks = spots.shape[0]
    share = width // blocks
    for c in range(count):

        @pl.when(step == c * per)
        def _():
            for s in range(2):
                left = lefts[2 * c + s]
                for b in range(width // 128):
                    part = left[:, b * 128:(b + 1) * 128].T
                    for t in range(128 // share):
                        spot = pl.multiple_of(spots[b * (128 // share) + t] * share, share)
                        turned[pl.ds(spot, share), s * rows:(s + 1) * rows] = part[t * share:(t + 1) * share]

    def tile(right_a, right_b):
        return (dot(turned[:, :rows], right_a[...]) + dot(turned[:, rows:], right_b[...])).astype(BF16)

    quarter = width // 8

    def put(value):
        @pl.when(step < half)
        def _():
            left_kept[...] = value[: width // 2]
            left_sent[...] = value[width // 2:]

        @pl.when(step >= half)
        def _():
            for a, b in enumerate(quarters):
                right_kept[a * quarter:(a + 1) * quarter] = value[b * quarter:(b + 1) * quarter]
                right_sent[a * quarter:(a + 1) * quarter] = value[width // 2 + b * quarter:width // 2 + (b + 1) * quarter]

    if count == 1:
        put(tile(rights[0], rights[1]))
    else:
        for c in range(count):

            @pl.when(step // per == c)
            def _():
                put(tile(rights[2 * c], rights[2 * c + 1]))


def weight_grads(spots, quarters, lefts, rights, name):
    count = len(lefts)
    rows, width = lefts[0][0].shape
    columns = rights[0][0].shape[1] * count
    tile = 256
    steps = columns // tile
    per = steps // count
    half = steps // 2

    def right_spec(c):
        return pl.BlockSpec((rows, tile), lambda n, spots: (0, jnp.clip(n - c * per, 0, per - 1)))

    def out_spec(first):
        return pl.BlockSpec((width // 2, tile), lambda n, spots: (0, jnp.clip(n - first, 0, half - 1)))

    whole = pl.BlockSpec((rows, width), lambda n, spots: (0, 0))
    return pl.pallas_call(
        functools.partial(weight_kernel, count, half, quarters),
        out_shape=[jax.ShapeDtypeStruct((width // 2, columns // 2), BF16)] * 4,
        grid_spec=pltpu.PrefetchScalarGridSpec(
            num_scalar_prefetch=1,
            grid=(steps,),
            in_specs=[whole] * (2 * count) + [right_spec(c) for c in range(count) for _ in range(2)],
            out_specs=[out_spec(0), out_spec(0), out_spec(half), out_spec(half)],
            scratch_shapes=[pltpu.VMEM((width, 2 * rows), BF16)],
        ),
        compiler_params=pltpu.CompilerParams(vmem_limit_bytes=VMEM_LIMIT),
        cost_estimate=pl.CostEstimate(flops=4 * rows * width * columns, bytes_accessed=24 << 20, transcendentals=0),
        name=name,
    )(spots, *[a for pair in lefts for a in pair], *[a for pair in rights for a in pair])


def bits_of(extent):
    return [1 << i for i in range(extent.bit_length() - 1)]


def exchange(values, axis, bit):
    extent = lax.axis_size(axis)
    return lax.ppermute(values, axis, [(i, i ^ bit) for i in range(extent)])


def reduce_steps(kept, sent, order, share):
    columns = kept.shape[-1]
    kept = kept.reshape(-1, share, columns)
    sent = sent.reshape(-1, share, columns)
    for i, (axis, bit) in enumerate(order):
        total = kept.astype(F32) + exchange(sent, axis, bit).astype(F32)
        if i < len(order) - 1:
            middle = total.shape[0] // 2
            kept, sent = total[:middle], total[middle:].astype(BF16)
    return total[0]


def local(
    latents, cotangent, slot_crops, ln1_scale, ln1_offset, qkv_weight, out_weight, out_bias,
    ln2_scale, ln2_offset, up_weight, up_bias, down_weight, down_bias,
):
    slots, chunk, width = latents.shape
    images, lanes = lax.axis_size("img"), lax.axis_size("row")
    row = lax.axis_index("row")
    rounds = slots // lanes
    share = jnp.where(slot_crops > 0, 1.0 / jnp.maximum(slot_crops, 1).astype(F32), 0.0)

    def gather(values):
        blocks = values.reshape(rounds, lanes, chunk, width)
        got = []
        for k in range(lanes):
            mine = lax.dynamic_index_in_dim(blocks, row ^ k, 1, keepdims=False)
            got.append(mine if k == 0 else exchange(mine, "row", k))
        return got

    xs = gather(latents)
    cots = gather(cotangent)
    as_row = lambda v: v.reshape(1, -1)
    vecs = [as_row(v) for v in (ln1_scale, ln1_offset, ln2_scale, ln2_offset, out_bias, up_bias, down_bias)]
    mats = [qkv_weight, out_weight, up_weight, down_weight]
    saved, outs, grads, sums, wgs = [], [], [], [], []
    for r in range(rounds):
        full = lax.dynamic_slice(slot_crops, (r * lanes + row,), (1,))
        out, keep = forward(full, [x[r] for x in xs], vecs, mats)
        outs.append(out)
        saved.append(keep)
    for r in range(rounds):
        part = lax.dynamic_slice(share, (r * lanes + row,), (1,))
        h1, qkv, probs, mixed, resid, h2, pre, act = saved[r]
        grad, total, wg = backward(
            part, [c[r] for c in cots], [x[r] for x in xs], [vecs[0], vecs[2]],
            [down_weight, pre, up_weight, resid, out_weight, qkv, probs, qkv_weight, qkv_weight],
        )
        grads.append(grad)
        sums.append(total)
        wgs.append(wg)

    def scatter(pieces):
        back = []
        for k in range(lanes):
            mine = jnp.stack([pieces[r][k] for r in range(rounds)])
            back.append(mine if k == 0 else exchange(mine, "row", k))
        both = jnp.stack(back, 1)
        order = jnp.arange(lanes) ^ row
        return jnp.take(both, order, axis=1).reshape(slots, chunk, width)

    block_out = scatter(outs)
    latents_grad = scatter(grads)

    devices = images * lanes
    me = lax.axis_index("img") * lanes + row
    core, others = 1, bits_of(images)[1:]
    plan = [("img", core)] + [("img", b) for b in others] + [("row", b) for b in bits_of(lanes)]
    turned_plan = [("img", core)] + [("img", b) for b in reversed(others)] + [("row", b) for b in bits_of(lanes)]
    rows_of = width // devices
    relative = jnp.arange(devices, dtype=jnp.int32) ^ me

    def places(steps):
        spots = jnp.zeros_like(relative)
        for axis, bit in steps:
            spots = spots * 2 + (relative // (bit * lanes if axis == "img" else bit)) % 2
        return spots

    in_kernel = rows_of % 16 == 0 and len(others) == 2
    if in_kernel:
        spots, quarters = places(plan), (0, 2, 1, 3)
    else:
        spots, quarters = jnp.arange(width // 128, dtype=jnp.int32), (0, 1, 2, 3)
    pair = lambda index: [wgs[r][index] for r in range(rounds)]
    keep = lambda index: [saved[r][index] for r in range(rounds)]
    first = weight_grads(spots, quarters, [keep(7), keep(5), keep(3)], [pair(0), pair(1), pair(2)], "weights_first")
    second = weight_grads(spots, quarters, [keep(0)], [pair(3)], "weights_second")

    def arranged(kept, sent, steps):
        if in_kernel:
            return kept, sent
        natural = jnp.concatenate([kept, sent]).reshape(devices, rows_of, -1)
        placed = jnp.take(natural, jnp.argsort(places(steps)), axis=0)
        return placed[: devices // 2], placed[devices // 2:]

    def finish(parts):
        halves = []
        for kept, sent, steps in ((parts[0], parts[1], plan), (parts[2], parts[3], turned_plan)):
            halves.append(reduce_steps(*arranged(kept, sent, steps), steps, rows_of))
        return jnp.concatenate(halves, 1)

    mlp = finish(first)
    qkv_grad = finish(second)
    total = lax.psum_scatter(sum(sums), ("img", "row"), scatter_dimension=1, tiled=True)
    down_grad, up_grad, out_grad = jnp.split(mlp, 3, 1)
    return (
        block_out, latents_grad, total[5], total[6], qkv_grad, out_grad, total[4], total[2], total[3],
        up_grad, total[1], down_grad, total[0],
    )


def solution(mesh):
    whole, both = P(), P(("img", "row"))
    rows, wide = P("img", "row", None), P(("img", "row"), None)
    in_specs = (rows, rows, P("img")) + (whole,) * 11
    out_specs = (rows, rows, both, both, wide, wide, both, both, both, wide, both, wide, both)
    return jax.shard_map(local, mesh=mesh, in_specs=in_specs, out_specs=out_specs, check_vma=False)
```

time: 1370 us -> 500 us (0.36)
  waiting for transfers between devices: 1020 us -> 219 us
  matrix products: 142 us -> 0 us
  Pallas kernels: 0 us -> 138 us
  starting transfers between devices: 0.71 us -> 64.2 us
  local copies, waits for them, and re-layouts: 92.9 us -> 37.6 us
  blocking collectives: 42.2 us -> 0 us
  other arithmetic: 53.4 us -> 21.7 us
    reduce_scatter x4 -> x0, waiting for transfers between devices: 507 us -> none  [the longest x1 162 us: local(): lax.psum_scatter(qkv_grad, ('img', 'row'), scatter_dimension=0, tiled=True)]
    all_gather x2 -> x0, waiting for transfers between devices: 273 us -> none  [the longest x1 137 us: local(): lax.all_gather(value_local, 'row', axis=1, tiled=True)]
    pallas_call x0 -> x6, Pallas kernels: none -> 138 us  [the longest x2 59.7 us: backward(): pl.pallas_call(functools.partial(backward_kernel, pieces, rows, width), o...]
    dot_general x17 -> x0, matrix products: 129 us -> none  [the longest x4 33.6 us: outer_total(): lax.dot_general(left, right, (((0,), (0,)), ((), ())), preferred_element_...]
    unnamed x8 -> x2, waiting for transfers between devices: 240 us -> 119 us
    ppermute x0 -> x32, waiting for transfers between devices: none -> 100 us  [exchange(): return lax.ppermute(values, axis, [(i, i ^ bit) for i in range(extent)])]
    ppermute x0 -> x32, starting transfers between devices: none -> 64.1 us  [exchange(): return lax.ppermute(values, axis, [(i, i ^ bit) for i in range(extent)])]
    unnamed x99 -> x72, local copies, waits for them, and re-layouts: 50.9 us -> 7.6 us
  transfers between devices with their start and end apart: 7 -> 33, of which waited for: 7 -> 15; matrix products, arithmetic and copies ran while one was open for 9% -> 11% of each run, Pallas kernels for 0% -> 12%
where the time goes in v1:
time: 500 us; the launch traced here: 496 us
  waiting for transfers between devices  219 us (44%)
  Pallas kernels  138 us (28%)
  starting transfers between devices  64.2 us (13%)
  local copies, waits for them, and re-layouts  37.6 us (8%)
  other arithmetic  21.7 us (4%)
  between operations  15.3 us (3%)
    unnamed x2, waiting for transfers between devices  119 us
    ppermute x32, waiting for transfers between devices, exchange(): return lax.ppermute(values, axis, [(i, i ^ bit) for i in range(extent)])  100 us
    ppermute x32, starting transfers between devices, exchange(): return lax.ppermute(values, axis, [(i, i ^ bit) for i in range(extent)])  64.1 us
    pallas_call x2, Pallas kernels, backward(): pl.pallas_call(functools.partial(backward_kernel, pieces, rows, width), o...  59.7 us
    pallas_call x2, Pallas kernels, forward(): pl.pallas_call(functools.partial(forward_kernel, pieces, rows, width), ou...  43.7 us
    pallas_call x2, Pallas kernels, weight_grads(): pl.pallas_call(functools.partial(weight_kernel, count, half, quarters), o...  35 us
  transfers between devices with their start and end apart: 33, of which 15 were waited for; matrix products, arithmetic and copies ran while one was open for 11% of the time, Pallas kernels for 12%

profile of v1, /device:TPU:0, one launch (start us, length us, event | category | flops | bytes accessed | tf_op | source)
XLA Modules:
  0.0 496.2 jit_solution(8951578939321954899)
XLA Ops:
  7.3 2.7 dynamic-slice_bitcast_fusion.3
  10.0 5.0 %collective-permute-start.2 = (bf16[2,128,1024]{2,1,0:T(8,128)(2,1)}, bf16[2,128,1024]{2,1,0:T(8,128)(2,1)}, u32[]{:S(2)}, u32[]{:S(2)}) collective-permute-start(bf16[2,128,1024]{2,1,0:T(8,128)(2,1)} %get-tuple-element.121), channel_id=1, source_target_pairs={{0,3},{1,2},{2,1},{3,0},{4,7},{5,6},{6,5},{7,4},{8,11},{9,10},{10,... | collective-permute-start | bytes 1572872 | tf_op jit(solution)/shard_map/ppermute | solution.py:373
  16.6 3.8 collective-permute-start.8
  20.5 2.0 dynamic-slice_bitcast_fusion.7
  28.4 22.8 %collective-permute-start.6 = (bf16[2,128,1024]{2,1,0:T(8,128)(2,1)S(1)}, bf16[2,128,1024]{2,1,0:T(8,128)(2,1)S(1)}, u32[]{:S(2)}, u32[]{:S(2)}) collective-permute-start(bf16[2,128,1024]{2,1,0:T(8,128)(2,1)S(1)} %get-tuple-element.118), channel_id=1, source_target_pairs={{0,1},{1,0},{2,3},{3,2},{4,5},{5,4},{6,7},{7,6},{8,9},{9,8},{10,11... | collective-permute-start | bytes 1572872 | tf_op jit(solution)/shard_map/ppermute | solution.py:373
  51.2 1.9 slice_bitcast_fusion.9
  53.1 30.4 %collective-permute-done.1 = bf16[2,128,1024]{2,1,0:T(8,128)(2,1)} collective-permute-done((bf16[2,128,1024]{2,1,0:T(8,128)(2,1)}, bf16[2,128,1024]{2,1,0:T(8,128)(2,1)}, u32[]{:S(2)}, u32[]{:S(2)}) %collective-permute-start.1) | collective-permute-done | bytes 524320 | tf_op jit(solution)/shard_map/ppermute | solution.py:373
  85.4 1.9 slice_bitcast_fusion.11
  87.3 1.9 slice_bitcast_fusion.3
  89.2 21.8 %slot_forward.2 = (bf16[128,1024]{1,0:T(8,128)(2,1)}, bf16[128,1024]{1,0:T(8,128)(2,1)}, bf16[128,1024]{1,0:T(8,128)(2,1)}, bf16[128,1024]{1,0:T(8,128)(2,1)}, b...) custom-call(s32[1]{0:T(128)} %get-tuple-element.150.refs_0_, ...), custom_call_target="tpu_custom_call" | custom-call | flops 7516192768 | bytes 33554432 | tf_op jit(solution)/shard_map/slot_forward/pallas_call | solution.py:137
  111.0 1.9 slice_bitcast_fusion.4
  112.9 21.9 %slot_forward.3 = (bf16[128,1024]{1,0:T(8,128)(2,1)}, bf16[128,1024]{1,0:T(8,128)(2,1)}, bf16[128,1024]{1,0:T(8,128)(2,1)}, bf16[128,1024]{1,0:T(8,128)(2,1)}, b...) custom-call(s32[1]{0:T(128)} %get-tuple-element.151.refs_0_, ...), custom_call_target="tpu_custom_call" | custom-call | flops 7516192768 | bytes 33554432 | tf_op jit(solution)/shard_map/slot_forward/pallas_call | solution.py:137
  135.6 30.0 %slot_backward.2 = (bf16[128,1024]{1,0:T(8,128)(2,1)}, bf16[128,1024]{1,0:T(8,128)(2,1)}, bf16[128,1024]{1,0:T(8,128)(2,1)}, bf16[128,1024]{1,0:T(8,128)(2,1)}, ...) custom-call(f32[1]{0:T(128)} %get-tuple-element.148.refs_0_, ...), custom_call_target="tpu_custom_call" | custom-call | flops 8589934592 | bytes 33554432 | tf_op jit(solution)/shard_map/slot_backward/pallas_call | solution.py:270
  165.6 29.7 %slot_backward.3 = (bf16[128,1024]{1,0:T(8,128)(2,1)}, bf16[128,1024]{1,0:T(8,128)(2,1)}, bf16[128,1024]{1,0:T(8,128)(2,1)}, bf16[128,1024]{1,0:T(8,128)(2,1)}, ...) custom-call(f32[1]{0:T(128)} %get-tuple-element.149.refs_0_, ...), custom_call_target="tpu_custom_call" | custom-call | flops 8589934592 | bytes 33554432 | tf_op jit(solution)/shard_map/slot_backward/pallas_call | solution.py:270
  195.3 18.9 %weights_first.1 = (bf16[512,1536]{1,0:T(8,128)(2,1)}, bf16[512,1536]{1,0:T(8,128)(2,1)}, bf16[512,1536]{1,0:T(8,128)(2,1)}, bf16[512,1536]{1,0:T(8,128)(2,1)}) custom-call(s32[32]{0:T(128)} %fusion.7.refs_0_, bf16[512,1024]{1,0:T(8,128)(2,1)} %get-tuple-element.98.refs_1_, bf16[512,1024]{1,0:T(8,128)(2,1)} %get-tuple-element.99.refs_2_, ...), custom_call_target="tpu_custom_call" | custom-call | flops 6442450944 | bytes 25165824 | tf_op jit(solution)/shard_map/weights_first/pallas_call | solution.py:351
  215.6 8.1 %collective-permute-start.3 = (bf16[2,128,1024]{2,1,0:T(8,128)(2,1)S(1)}, bf16[2,128,1024]{2,1,0:T(8,128)(2,1)S(1)}, u32[]{:S(2)}, u32[]{:S(2)}) collective-permute-start(bf16[2,128,1024]{2,1,0:T(8,128)(2,1)S(1)} %pad_maximum_fusion.2), channel_id=1, source_target_pairs={{0,1},{1,0},{2,3},{3,2},{4,5},{5,4},{6,7},{7,6},{8,9},{9,8},{10,11... | collective-permute-start | bytes 1572872 | tf_op jit(solution)/shard_map/ppermute | solution.py:373
  231.1 16.1 %weights_second.1 = (bf16[512,1536]{1,0:T(8,128)(2,1)}, bf16[512,1536]{1,0:T(8,128)(2,1)}, bf16[512,1536]{1,0:T(8,128)(2,1)}, bf16[512,1536]{1,0:T(8,128)(2,1)}) custom-call(s32[32]{0:T(128)} %fusion.7.refs_0_, bf16[512,1024]{1,0:T(8,128)(2,1)} %get-tuple-element.90.refs_1_, bf16[512,1024]{1,0:T(8,128)(2,1)} %get-tuple-element.91.refs_2_, ...), custom_call_target="tpu_custom_call" | custom-call | flops 6442450944 | bytes 25165824 | tf_op jit(solution)/shard_map/weights_second/pallas_call | solution.py:351
  249.4 14.2 %collective-permute-done.4 = bf16[2,128,1024]{2,1,0:T(8,128)(2,1)S(1)} collective-permute-done((bf16[2,128,1024]{2,1,0:T(8,128)(2,1)S(1)}, bf16[2,128,1024]{2,1,0:T(8,128)(2,1)S(1)}, u32[]{:S(2)}, u32[]{:S(2)}) %collective-permute-start.4) | collective-permute-done | bytes 524320 | tf_op jit(solution)/shard_map/ppermute | solution.py:373
  263.6 2.6 collective-permute-start.11
  267.4 118.7 %reduce-scatter.4.cloned.1.call-done = f32[32,8]{1,0:T(8,128)} async-done(((f32[1024,8]{1,0:T(8,128)}), f32[32,8]{1,0:T(8,128)}) %reduce-scatter.4.cloned.1.call-update) | async-done | bytes 1040
  392.8 2.0 gather_fusion
  397.0 2.0 gather_fusion.1
  399.0 2.7 select_bitcast_fusion
  418.7 8.9 %collective-permute-done.23 = bf16[8,32,1536]{2,1,0:T(8,128)(2,1)S(1)} collective-permute-done((bf16[8,32,1536]{2,1,0:T(8,128)(2,1)S(1)}, bf16[8,32,1536]{2,1,0:T(8,128)(2,1)S(1)}, u32[]{:S(2)}, u32[]{:S(2)}) %collective-permute-start.23) | collective-permute-done | bytes 786464 | tf_op jit(solution)/shard_map/ppermute | solution.py:373
  428.0 3.4 collective-permute-done.28
  432.9 15.3 %collective-permute-done.13 = bf16[8,32,1536]{2,1,0:T(8,128)(2,1)S(1)} collective-permute-done((bf16[8,32,1536]{2,1,0:T(8,128)(2,1)S(1)}, bf16[8,32,1536]{2,1,0:T(8,128)(2,1)S(1)}, u32[]{:S(2)}, u32[]{:S(2)}) %collective-permute-start.13) | collective-permute-done | bytes 786464 | tf_op jit(solution)/shard_map/ppermute | solution.py:373
  450.1 6.5 %collective-permute-done.24 = bf16[4,32,1536]{2,1,0:T(8,128)(2,1)S(1)} collective-permute-done((bf16[4,32,1536]{2,1,0:T(8,128)(2,1)S(1)}, bf16[4,32,1536]{2,1,0:T(8,128)(2,1)S(1)}, u32[]{:S(2)}, u32[]{:S(2)}) %collective-permute-start.24) | collective-permute-done | bytes 393248 | tf_op jit(solution)/shard_map/ppermute | solution.py:373
  461.7 2.2 collective-permute-done.19
  465.2 2.9 collective-permute-start.26
  469.8 7.3 %collective-permute-done.15 = bf16[2,32,1536]{2,1,0:T(8,128)(2,1)S(1)} collective-permute-done((bf16[2,32,1536]{2,1,0:T(8,128)(2,1)S(1)}, bf16[2,32,1536]{2,1,0:T(8,128)(2,1)S(1)}, u32[]{:S(2)}, u32[]{:S(2)}) %collective-permute-start.15) | collective-permute-done | bytes 196640 | tf_op jit(solution)/shard_map/ppermute | solution.py:373
  477.3 2.0 collective-permute-done.20
  480.4 6.6 %collective-permute-done.16 = bf16[1,32,1536]{2,1,0:T(8,128)(2,1)S(1)} collective-permute-done((bf16[1,32,1536]{2,1,0:T(8,128)(2,1)S(1)}, bf16[1,32,1536]{2,1,0:T(8,128)(2,1)S(1)}, u32[]{:S(2)}, u32[]{:S(2)}) %collective-permute-start.16) | collective-permute-done | bytes 98336 | tf_op jit(solution)/shard_map/ppermute | solution.py:373
  (191 shorter events, 62.8 us)
Async XLA Ops:
  7.2 378.9 %reduce-scatter.4.cloned.1.call-start = ((), (), s32[]{:S(2)}) async-start(), calls=%async_computation.1 | async-start | bytes 540672
  10.0 18.5 %collective-permute-start.2 = (bf16[2,128,1024]{2,1,0:T(8,128)(2,1)}, bf16[2,128,1024]{2,1,0:T(8,128)(2,1)}, u32[]{:S(2)}, u32[]{:S(2)}) collective-permute-start(bf16[2,128,1024]{2,1,0:T(8,128)(2,1)} %get-tuple-element.121), channel_id=1, source_target_pairs={{0,3},{1,2},{2,1},{3,0},{4,7},{5,6},{6,5},{7,4},{8,11},{9,10},{10,... | collective-permute-start | bytes 1572872 | tf_op jit(solution)/shard_map/ppermute | solution.py:373
  15.0 68.5 %collective-permute-start.1 = (bf16[2,128,1024]{2,1,0:T(8,128)(2,1)}, bf16[2,128,1024]{2,1,0:T(8,128)(2,1)}, u32[]{:S(2)}, u32[]{:S(2)}) collective-permute-start(bf16[2,128,1024]{2,1,0:T(8,128)(2,1)} %get-tuple-element.122), channel_id=1, source_target_pairs={{0,2},{1,3},{2,0},{3,1},{4,6},{5,7},{6,4},{7,5},{8,10},{9,11},{10,... | collective-permute-start | bytes 1572872 | tf_op jit(solution)/shard_map/ppermute | solution.py:373
  15.0 70.4 %collective-permute-start = (bf16[2,128,1024]{2,1,0:T(8,128)(2,1)}, bf16[2,128,1024]{2,1,0:T(8,128)(2,1)}, u32[]{:S(2)}, u32[]{:S(2)}) collective-permute-start(bf16[2,128,1024]{2,1,0:T(8,128)(2,1)} %get-tuple-element.123), channel_id=1, source_target_pairs={{0,1},{1,0},{2,3},{3,2},{4,5},{5,4},{6,7},{7,6},{8,9},{9,8},{10,11... | collective-permute-start | bytes 1572872 | tf_op jit(solution)/shard_map/ppermute | solution.py:373
  16.6 70.6 %collective-permute-start.8 = (bf16[2,128,1024]{2,1,0:T(8,128)(2,1)}, bf16[2,128,1024]{2,1,0:T(8,128)(2,1)}, u32[]{:S(2)}, u32[]{:S(2)}) collective-permute-start(bf16[2,128,1024]{2,1,0:T(8,128)(2,1)} %get-tuple-element.116), channel_id=1, source_target_pairs={{0,3},{1,2},{2,1},{3,0},{4,7},{5,6},{6,5},{7,4},{8,11},{9,10},{10,... | collective-permute-start | bytes 1572872 | tf_op jit(solution)/shard_map/ppermute | solution.py:373
  20.5 90.5 %collective-permute-start.7 = (bf16[2,128,1024]{2,1,0:T(8,128)(2,1)S(1)}, bf16[2,128,1024]{2,1,0:T(8,128)(2,1)}, u32[]{:S(2)}, u32[]{:S(2)}) collective-permute-start(bf16[2,128,1024]{2,1,0:T(8,128)(2,1)S(1)} %get-tuple-element.117), channel_id=1, source_target_pairs={{0,2},{1,3},{2,0},{3,1},{4,6},{5,7},{6,4},{7,5},{8,10},{9,11},{10,... | collective-permute-start | bytes 1572872 | tf_op jit(solution)/shard_map/ppermute | solution.py:373
  28.4 106.3 %collective-permute-start.6 = (bf16[2,128,1024]{2,1,0:T(8,128)(2,1)S(1)}, bf16[2,128,1024]{2,1,0:T(8,128)(2,1)S(1)}, u32[]{:S(2)}, u32[]{:S(2)}) collective-permute-start(bf16[2,128,1024]{2,1,0:T(8,128)(2,1)S(1)} %get-tuple-element.118), channel_id=1, source_target_pairs={{0,1},{1,0},{2,3},{3,2},{4,5},{5,4},{6,7},{7,6},{8,9},{9,8},{10,11... | collective-permute-start | bytes 1572872 | tf_op jit(solution)/shard_map/ppermute | solution.py:373
  214.3 190.3 %collective-permute-start.22 = (bf16[16,32,1536]{2,1,0:T(8,128)(2,1)}, bf16[16,32,1536]{2,1,0:T(8,128)(2,1)}, u32[]{:S(2)}, u32[]{:S(2)}) collective-permute-start(bf16[16,32,1536]{2,1,0:T(8,128)(2,1)} %bitcast.146), channel_id=1, source_target_pairs={{0,4},{4,0},{8,12},{12,8},{16,20},{20,16},{24,28},{28,24},{1,5},{5... | collective-permute-start | bytes 4718600 | tf_op jit(solution)/shard_map/ppermute | solution.py:373
  215.6 33.0 %collective-permute-start.3 = (bf16[2,128,1024]{2,1,0:T(8,128)(2,1)S(1)}, bf16[2,128,1024]{2,1,0:T(8,128)(2,1)S(1)}, u32[]{:S(2)}, u32[]{:S(2)}) collective-permute-start(bf16[2,128,1024]{2,1,0:T(8,128)(2,1)S(1)} %pad_maximum_fusion.2), channel_id=1, source_target_pairs={{0,1},{1,0},{2,3},{3,2},{4,5},{5,4},{6,7},{7,6},{8,9},{9,8},{10,11... | collective-permute-start | bytes 1572872 | tf_op jit(solution)/shard_map/ppermute | solution.py:373
  223.8 39.8 %collective-permute-start.4 = (bf16[2,128,1024]{2,1,0:T(8,128)(2,1)S(1)}, bf16[2,128,1024]{2,1,0:T(8,128)(2,1)S(1)}, u32[]{:S(2)}, u32[]{:S(2)}) collective-permute-start(bf16[2,128,1024]{2,1,0:T(8,128)(2,1)S(1)} %pad_maximum_fusion.3), channel_id=1, source_target_pairs={{0,2},{1,3},{2,0},{3,1},{4,6},{5,7},{6,4},{7,5},{8,10},{9,11},{10,... | collective-permute-start | bytes 1572872 | tf_op jit(solution)/shard_map/ppermute | solution.py:373
  225.1 42.1 %collective-permute-start.5 = (bf16[2,128,1024]{2,1,0:T(8,128)(2,1)S(1)}, bf16[2,128,1024]{2,1,0:T(8,128)(2,1)S(1)}, u32[]{:S(2)}, u32[]{:S(2)}) collective-permute-start(bf16[2,128,1024]{2,1,0:T(8,128)(2,1)S(1)} %pad_maximum_fusion.4), channel_id=1, source_target_pairs={{0,3},{1,2},{2,1},{3,0},{4,7},{5,6},{6,5},{7,4},{8,11},{9,10},{10,... | collective-permute-start | bytes 1572872 | tf_op jit(solution)/shard_map/ppermute | solution.py:373
  228.5 166.3 %collective-permute-start.9 = (bf16[2,128,1024]{2,1,0:T(8,128)(2,1)}, bf16[2,128,1024]{2,1,0:T(8,128)(2,1)}, u32[]{:S(2)}, u32[]{:S(2)}) collective-permute-start(bf16[2,128,1024]{2,1,0:T(8,128)(2,1)} %pad_maximum_fusion.5), channel_id=1, source_target_pairs={{0,1},{1,0},{2,3},{3,2},{4,5},{5,4},{6,7},{7,6},{8,9},{9,8},{10,11... | collective-permute-start | bytes 1572872 | tf_op jit(solution)/shard_map/ppermute | solution.py:373
  248.6 146.2 %collective-permute-start.10 = (bf16[2,128,1024]{2,1,0:T(8,128)(2,1)}, bf16[2,128,1024]{2,1,0:T(8,128)(2,1)}, u32[]{:S(2)}, u32[]{:S(2)}) collective-permute-start(bf16[2,128,1024]{2,1,0:T(8,128)(2,1)} %pad_maximum_fusion.6), channel_id=1, source_target_pairs={{0,2},{1,3},{2,0},{3,1},{4,6},{5,7},{6,4},{7,5},{8,10},{9,11},{10,... | collective-permute-start | bytes 1572872 | tf_op jit(solution)/shard_map/ppermute | solution.py:373
  263.6 131.7 %collective-permute-start.11 = (bf16[2,128,1024]{2,1,0:T(8,128)(2,1)}, bf16[2,128,1024]{2,1,0:T(8,128)(2,1)}, u32[]{:S(2)}, u32[]{:S(2)}) collective-permute-start(bf16[2,128,1024]{2,1,0:T(8,128)(2,1)} %pad_maximum_fusion.7), channel_id=1, source_target_pairs={{0,3},{1,2},{2,1},{3,0},{4,7},{5,6},{6,5},{7,4},{8,11},{9,10},{10,... | collective-permute-start | bytes 1572872 | tf_op jit(solution)/shard_map/ppermute | solution.py:373
  267.3 141.6 %collective-permute-start.27 = (bf16[16,32,1536]{2,1,0:T(8,128)(2,1)}, bf16[16,32,1536]{2,1,0:T(8,128)(2,1)}, u32[]{:S(2)}, u32[]{:S(2)}) collective-permute-start(bf16[16,32,1536]{2,1,0:T(8,128)(2,1)} %bitcast.145), channel_id=1, source_target_pairs={{0,4},{4,0},{8,12},{12,8},{16,20},{20,16},{24,28},{28,24},{1,5},{5... | collective-permute-start | bytes 4718600 | tf_op jit(solution)/shard_map/ppermute | solution.py:373
  394.8 16.1 %collective-permute-start.12 = (bf16[16,32,1536]{2,1,0:T(8,128)(2,1)}, bf16[16,32,1536]{2,1,0:T(8,128)(2,1)}, u32[]{:S(2)}, u32[]{:S(2)}) collective-permute-start(bf16[16,32,1536]{2,1,0:T(8,128)(2,1)} %bitcast.148), channel_id=1, source_target_pairs={{0,4},{4,0},{8,12},{12,8},{16,20},{20,16},{24,28},{28,24},{1,5},{5... | collective-permute-start | bytes 4718600 | tf_op jit(solution)/shard_map/ppermute | solution.py:373
  394.8 20.2 %collective-permute-start.17 = (bf16[16,32,1536]{2,1,0:T(8,128)(2,1)}, bf16[16,32,1536]{2,1,0:T(8,128)(2,1)}, u32[]{:S(2)}, u32[]{:S(2)}) collective-permute-start(bf16[16,32,1536]{2,1,0:T(8,128)(2,1)} %bitcast.147), channel_id=1, source_target_pairs={{0,4},{4,0},{8,12},{12,8},{16,20},{20,16},{24,28},{28,24},{1,5},{5... | collective-permute-start | bytes 4718600 | tf_op jit(solution)/shard_map/ppermute | solution.py:373
  407.2 20.5 %collective-permute-start.23 = (bf16[8,32,1536]{2,1,0:T(8,128)(2,1)S(1)}, bf16[8,32,1536]{2,1,0:T(8,128)(2,1)S(1)}, u32[]{:S(2)}, u32[]{:S(2)}) collective-permute-start(bf16[8,32,1536]{2,1,0:T(8,128)(2,1)S(1)} %slice.356), channel_id=1, source_target_pairs={{0,16},{4,20},{8,24},{12,28},{16,0},{20,4},{24,8},{28,12},{1,17},{... | collective-permute-start | bytes 2359304 | tf_op jit(solution)/shard_map/ppermute | solution.py:373
  410.9 20.5 %collective-permute-start.28 = (bf16[8,32,1536]{2,1,0:T(8,128)(2,1)S(1)}, bf16[8,32,1536]{2,1,0:T(8,128)(2,1)S(1)}, u32[]{:S(2)}, u32[]{:S(2)}) collective-permute-start(bf16[8,32,1536]{2,1,0:T(8,128)(2,1)S(1)} %slice.355), channel_id=1, source_target_pairs={{0,8},{4,12},{8,0},{12,4},{16,24},{20,28},{24,16},{28,20},{1,9},{5... | collective-permute-start | bytes 2359304 | tf_op jit(solution)/shard_map/ppermute | solution.py:373
  414.2 34.1 %collective-permute-start.13 = (bf16[8,32,1536]{2,1,0:T(8,128)(2,1)S(1)}, bf16[8,32,1536]{2,1,0:T(8,128)(2,1)S(1)}, u32[]{:S(2)}, u32[]{:S(2)}) collective-permute-start(bf16[8,32,1536]{2,1,0:T(8,128)(2,1)S(1)} %slice.358), channel_id=1, source_target_pairs={{0,8},{4,12},{8,0},{12,4},{16,24},{20,28},{24,16},{28,20},{1,9},{5... | collective-permute-start | bytes 2359304 | tf_op jit(solution)/shard_map/ppermute | solution.py:373
  417.4 32.3 %collective-permute-start.18 = (bf16[8,32,1536]{2,1,0:T(8,128)(2,1)S(1)}, bf16[8,32,1536]{2,1,0:T(8,128)(2,1)S(1)}, u32[]{:S(2)}, u32[]{:S(2)}) collective-permute-start(bf16[8,32,1536]{2,1,0:T(8,128)(2,1)S(1)} %slice.357), channel_id=1, source_target_pairs={{0,16},{4,20},{8,24},{12,28},{16,0},{20,4},{24,8},{28,12},{1,17},{... | collective-permute-start | bytes 2359304 | tf_op jit(solution)/shard_map/ppermute | solution.py:373
  427.9 28.7 %collective-permute-start.24 = (bf16[4,32,1536]{2,1,0:T(8,128)(2,1)S(1)}, bf16[4,32,1536]{2,1,0:T(8,128)(2,1)S(1)}, u32[]{:S(2)}, u32[]{:S(2)}) collective-permute-start(bf16[4,32,1536]{2,1,0:T(8,128)(2,1)S(1)} %slice.360), channel_id=1, source_target_pairs={{0,8},{4,12},{8,0},{12,4},{16,24},{20,28},{24,16},{28,20},{1,9},{5... | collective-permute-start | bytes 1179656 | tf_op jit(solution)/shard_map/ppermute | solution.py:373
  431.6 26.2 %collective-permute-start.29 = (bf16[4,32,1536]{2,1,0:T(8,128)(2,1)S(1)}, bf16[4,32,1536]{2,1,0:T(8,128)(2,1)S(1)}, u32[]{:S(2)}, u32[]{:S(2)}) collective-permute-start(bf16[4,32,1536]{2,1,0:T(8,128)(2,1)S(1)} %slice.359), channel_id=1, source_target_pairs={{0,16},{4,20},{8,24},{12,28},{16,0},{20,4},{24,8},{28,12},{1,17},{... | collective-permute-start | bytes 1179656 | tf_op jit(solution)/shard_map/ppermute | solution.py:373
  448.5 12.0 %collective-permute-start.14 = (bf16[4,32,1536]{2,1,0:T(8,128)(2,1)S(1)}, bf16[4,32,1536]{2,1,0:T(8,128)(2,1)S(1)}, u32[]{:S(2)}, u32[]{:S(2)}) collective-permute-start(bf16[4,32,1536]{2,1,0:T(8,128)(2,1)S(1)} %slice.362), channel_id=1, source_target_pairs={{0,16},{4,20},{8,24},{12,28},{16,0},{20,4},{24,8},{28,12},{1,17},{... | collective-permute-start | bytes 1179656 | tf_op jit(solution)/shard_map/ppermute | solution.py:373
  450.1 13.8 %collective-permute-start.19 = (bf16[4,32,1536]{2,1,0:T(8,128)(2,1)S(1)}, bf16[4,32,1536]{2,1,0:T(8,128)(2,1)S(1)}, u32[]{:S(2)}, u32[]{:S(2)}) collective-permute-start(bf16[4,32,1536]{2,1,0:T(8,128)(2,1)S(1)} %slice.361), channel_id=1, source_target_pairs={{0,8},{4,12},{8,0},{12,4},{16,24},{20,28},{24,16},{28,20},{1,9},{5... | collective-permute-start | bytes 1179656 | tf_op jit(solution)/shard_map/ppermute | solution.py:373
  458.0 10.6 %collective-permute-start.30 = (bf16[2,32,1536]{2,1,0:T(8,128)(2,1)S(1)}, bf16[2,32,1536]{2,1,0:T(8,128)(2,1)S(1)}, u32[]{:S(2)}, u32[]{:S(2)}) collective-permute-start(bf16[2,32,1536]{2,1,0:T(8,128)(2,1)S(1)} %slice.363), channel_id=1, source_target_pairs={{0,1},{1,0},{2,3},{3,2},{4,5},{5,4},{6,7},{7,6},{8,9},{9,8},{10,11... | collective-permute-start | bytes 589832 | tf_op jit(solution)/shard_map/ppermute | solution.py:373
  460.6 16.5 %collective-permute-start.15 = (bf16[2,32,1536]{2,1,0:T(8,128)(2,1)S(1)}, bf16[2,32,1536]{2,1,0:T(8,128)(2,1)S(1)}, u32[]{:S(2)}, u32[]{:S(2)}) collective-permute-start(bf16[2,32,1536]{2,1,0:T(8,128)(2,1)S(1)} %slice.366), channel_id=1, source_target_pairs={{0,1},{1,0},{2,3},{3,2},{4,5},{5,4},{6,7},{7,6},{8,9},{9,8},{10,11... | collective-permute-start | bytes 589832 | tf_op jit(solution)/shard_map/ppermute | solution.py:373
  464.0 15.2 %collective-permute-start.20 = (bf16[2,32,1536]{2,1,0:T(8,128)(2,1)S(1)}, bf16[2,32,1536]{2,1,0:T(8,128)(2,1)S(1)}, u32[]{:S(2)}, u32[]{:S(2)}) collective-permute-start(bf16[2,32,1536]{2,1,0:T(8,128)(2,1)S(1)} %slice.365), channel_id=1, source_target_pairs={{0,1},{1,0},{2,3},{3,2},{4,5},{5,4},{6,7},{7,6},{8,9},{9,8},{10,11... | collective-permute-start | bytes 589832 | tf_op jit(solution)/shard_map/ppermute | solution.py:373
  465.2 15.2 %collective-permute-start.26 = (bf16[1,32,1536]{2,1,0:T(8,128)(2,1)S(1)}, bf16[1,32,1536]{2,1,0:T(8,128)(2,1)S(1)}, u32[]{:S(2)}, u32[]{:S(2)}) collective-permute-start(bf16[1,32,1536]{2,1,0:T(8,128)(2,1)S(1)} %slice.368), channel_id=1, source_target_pairs={{0,2},{1,3},{2,0},{3,1},{4,6},{5,7},{6,4},{7,5},{8,10},{9,11},{10,... | collective-permute-start | bytes 294920 | tf_op jit(solution)/shard_map/ppermute | solution.py:373
  468.6 11.8 %collective-permute-start.31 = (bf16[1,32,1536]{2,1,0:T(8,128)(2,1)S(1)}, bf16[1,32,1536]{2,1,0:T(8,128)(2,1)S(1)}, u32[]{:S(2)}, u32[]{:S(2)}) collective-permute-start(bf16[1,32,1536]{2,1,0:T(8,128)(2,1)S(1)} %slice.367), channel_id=1, source_target_pairs={{0,2},{1,3},{2,0},{3,1},{4,6},{5,7},{6,4},{7,5},{8,10},{9,11},{10,... | collective-permute-start | bytes 294920 | tf_op jit(solution)/shard_map/ppermute | solution.py:373
  477.2 9.8 %collective-permute-start.16 = (bf16[1,32,1536]{2,1,0:T(8,128)(2,1)S(1)}, bf16[1,32,1536]{2,1,0:T(8,128)(2,1)S(1)}, u32[]{:S(2)}, u32[]{:S(2)}) collective-permute-start(bf16[1,32,1536]{2,1,0:T(8,128)(2,1)S(1)} %slice.370), channel_id=1, source_target_pairs={{0,2},{1,3},{2,0},{3,1},{4,6},{5,7},{6,4},{7,5},{8,10},{9,11},{10,... | collective-permute-start | bytes 294920 | tf_op jit(solution)/shard_map/ppermute | solution.py:373
  479.3 8.7 %collective-permute-start.21 = (bf16[1,32,1536]{2,1,0:T(8,128)(2,1)S(1)}, bf16[1,32,1536]{2,1,0:T(8,128)(2,1)S(1)}, u32[]{:S(2)}, u32[]{:S(2)}) collective-permute-start(bf16[1,32,1536]{2,1,0:T(8,128)(2,1)S(1)} %slice.369), channel_id=1, source_target_pairs={{0,2},{1,3},{2,0},{3,1},{4,6},{5,7},{6,4},{7,5},{8,10},{9,11},{10,... | collective-permute-start | bytes 294920 | tf_op jit(solution)/shard_map/ppermute | solution.py:373
  (33 other events, 708.7 us)
Sparse Core Ops, SparseCore 0:
  215.6 170.3 reduce-scatter.3
